TPU v7x, 32 devices: a whole 2x2x4 slice. The times are simulated.
32 devices in a mesh: row: 4 (over z), col: 2 (over y), win: 4 (over x, core).
Axes of the slice: x: 2, y: 2, z: 4, core: 2. Of those that a mesh axis runs over, the one named last changes fastest.
Arguments:
- counts: int32 [8, 512, 2048], P('win', 'row', 'col'), may hold values from 0 to 31, as said below
- row_factors: float32 [32, 512], P(None, ('row', 'col', 'win')), may hold values from 0.15 to 1.5
- col_factors: float32 [32, 2048], P(None, ('col', 'row', 'win')), may hold values from 0.15 to 1.5
- win_factors: float32 [32, 8], P(None, 'win'), may hold values from 0.15 to 1.5
Outputs:
- new_rows: float32 [32, 512], P(None, ('row', 'col', 'win'))
- new_cols: float32 [32, 2048], P(None, ('col', 'row', 'win'))
- new_wins: float32 [32, 8], P(None, 'win')
Inputs may be any that keep to these rules, and one draw needn't show every extreme that they name: counts are whole numbers.
All inputs are finite; a program needn't handle non-finite values.
Results may differ from a plain program's by a relative error of at most 0.0001.
Values sent between devices are 32-bit elements; how exact they have to be, the bound alone decides.
A program may use at most 64 MiB of HBM per device.

v0:
```python
import jax
import jax.numpy as jnp
from jax import lax
from jax.sharding import PartitionSpec as P

STEPS = 4


HIGH = lax.Precision.HIGHEST


def fetch_blocks(row_shard, col_shard):
    row_block = lax.all_gather(row_shard, ("col", "win"), axis=1, tiled=True)
    col_block = lax.all_gather(col_shard, ("row", "win"), axis=1, tiled=True)
    return (row_block, col_block)


def block_terms(counts, row_block, col_block, win_block):
    row_terms = jnp.zeros(row_block.shape, jnp.float32)
    col_terms = jnp.zeros(col_block.shape, jnp.float32)
    win_list = []
    for window in range(counts.shape[0]):
        weight = win_block[:, window : window + 1]
        scaled = row_block * weight
        model_block = lax.dot_general(
            scaled,
            col_block,
            (((0,), (0,)), ((), ())),
            precision=HIGH,
            preferred_element_type=jnp.float32,
        )
        count_ratio = counts[window].astype(jnp.float32) / model_block
        back_terms = lax.dot_general(
            col_block,
            count_ratio,
            (((1,), (1,)), ((), ())),
            precision=HIGH,
            preferred_element_type=jnp.float32,
        )
        row_terms = row_terms + back_terms * weight
        col_terms = col_terms + jnp.dot(
            scaled, count_ratio, precision=HIGH, preferred_element_type=jnp.float32
        )
        win_list.append(win_block[:, window] * jnp.sum(row_block * back_terms, axis=1))
    return (row_terms, col_terms, jnp.stack(win_list, axis=1))


def local(counts, row_factors, col_factors, win_factors):
    row_shard = row_factors
    col_shard = col_factors
    win_block = win_factors
    rank_count = row_shard.shape[0]
    win_count = counts.shape[0]
    all_windows = win_count * lax.axis_size("win")
    win_start = lax.axis_index("win") * win_count
    lead_mask = jnp.logical_and(lax.axis_index("row") == 0, lax.axis_index("col") == 0).astype(
        jnp.float32
    )
    row_block, col_block = fetch_blocks(row_shard, col_shard)
    for step_index in range(STEPS):
        row_terms, col_terms, win_terms = block_terms(counts, row_block, col_block, win_block)
        placed = lax.dynamic_update_slice(
            jnp.zeros((rank_count, all_windows), jnp.float32), win_terms, (jnp.int32(0), win_start)
        )
        sum_rows, sum_cols, sum_wins, win_total = lax.psum(
            (
                jnp.sum(row_shard, axis=1),
                jnp.sum(col_shard, axis=1),
                jnp.sum(win_block, axis=1) * lead_mask,
                placed,
            ),
            ("row", "col", "win"),
        )
        own_wins = lax.dynamic_slice(win_total, (jnp.int32(0), win_start), (rank_count, win_count))
        row_scale = (sum_cols * sum_wins)[:, None]
        col_scale = (sum_rows * sum_wins)[:, None]
        win_block = win_block * (0.5 + 0.5 * own_wins / (sum_rows * sum_cols)[:, None])
        row_sum = lax.psum_scatter(row_terms, ("col", "win"), scatter_dimension=1, tiled=True)
        col_sum = lax.psum_scatter(col_terms, ("row", "win"), scatter_dimension=1, tiled=True)
        row_shard = row_shard * (0.5 + 0.5 * row_sum / row_scale)
        col_shard = col_shard * (0.5 + 0.5 * col_sum / col_scale)
        if step_index + 1 < STEPS:
            row_block, col_block = fetch_blocks(row_shard, col_shard)
    return (row_shard, col_shard, win_block)


def solution(mesh):
    in_specs = (
        P("win", "row", "col"),
        P(None, ("row", "col", "win")),
        P(None, ("col", "row", "win")),
        P(None, "win"),
    )
    out_specs = (P(None, ("row", "col", "win")), P(None, ("col", "row", "win")), P(None, "win"))
    return jax.shard_map(local, mesh=mesh, in_specs=in_specs, out_specs=out_specs, check_vma=False)
```

profile of v0, /device:TPU:0, one launch (start us, length us, event | category | flops | bytes accessed | tf_op | source)
XLA Modules:
  0.0 501.9 jit_solution(4040150309405167772)
XLA Ops:
  7.2 10.8 %all_gather.24 = f32[32,128]{0,1:T(8,128)S(1)} all-gather(f32[32,16]{0,1:T(8,128)} %param.5), channel_id=1, replica_groups=mesh['row'=4,'col'=2,'win'=4] {'col','win'}, dimensions={1}, use_global_device_ids=true | all-gather | bytes 18432 | tf_op jit(solution)/shard_map/all_gather | solution.py:13
  18.1 0.7 copy-done
  18.8 22.2 %all-gather = f32[16,64,32]{1,2,0:T(8,128)S(1)} all-gather(f32[1,64,32]{1,2,0:T(8,128)S(1)} %bitcast.125), channel_id=1, replica_groups=mesh['row'=4,'col'=2,'win'=4] {'row','win'}, dimensions={0}, use_global_device_ids=true | all-gather | bytes 139264 | tf_op jit(solution)/shard_map/all_gather | solution.py:14
  41.2 0.5 copy-done.2
  41.8 0.7 convolution_divide_fusion.6
  42.5 0.6 convolution_bitcast_fusion
  43.1 0.7 convolution_divide_fusion.7
  43.9 0.7 multiply_reduce_fusion.7
  44.6 0.7 copy.42
  45.4 0.4 fusion.17
  45.8 0.4 convolution_add_fusion.3
  46.2 1.0 copy.44
  47.4 0.7 copy-done.1
  48.2 36.9 %all-reduce.3 = (f32[32]{0:T(128)S(1)}, f32[32]{0:T(128)S(1)}, f32[32]{0:T(128)S(1)}, f32[32,8]{0,1:T(8,128)S(1)}) all-reduce(f32[32]{0:T(128)S(1)} %reduce_sum.196, f32[32]{0:T(128)S(1)} %broadcast_multiply_fusion.3, f32[32]{0:T(128)S(1)} %reduce_sum.198, ...), channel_id=1, replica_groups=mesh['row'=4,'col'=2,'win'=4] {'row','col','win'}, use_global_device_ids=true, to_apply=%region_2.0 | all-reduce | flops 352 | bytes 2816 | tf_op jit(solution)/shard_map/psum | solution.py:65
  85.2 0.8 copy.43
  86.2 10.0 %all_gather.27 = f32[32,128]{0,1:T(8,128)S(1)} all-gather(f32[32,16]{0,1:T(8,128)S(1)} %copy.22), channel_id=1, replica_groups=mesh['row'=4,'col'=2,'win'=4] {'col','win'}, dimensions={1}, use_global_device_ids=true | all-gather | bytes 18432 | tf_op jit(solution)/shard_map/all_gather | solution.py:13
  96.3 38.7 %reduce-scatter.27.cloned.1.call-done = f32[64,32]{1,0:T(8,128)} async-done(((f32[1024,32]{1,0:T(8,128)}), f32[64,32]{1,0:T(8,128)}) %reduce-scatter.27.cloned.1.call-update) | async-done | bytes 8208
  135.0 0.8 copy.45
  135.8 0.2 fusion.52
  136.0 20.1 %all-gather.1 = f32[16,64,32]{1,2,0:T(8,128)S(1)} all-gather(f32[1,64,32]{1,2,0:T(8,128)S(1)} %bitcast.123), channel_id=1, replica_groups=mesh['row'=4,'col'=2,'win'=4] {'row','win'}, dimensions={0}, use_global_device_ids=true | all-gather | bytes 139264 | tf_op jit(solution)/shard_map/all_gather | solution.py:14
  156.4 0.7 convolution_divide_fusion.4
  157.1 0.6 fusion.57
  157.8 0.7 convolution_divide_fusion.5
  158.5 0.4 fusion.12
  158.9 0.7 multiply_reduce_fusion.5
  159.6 0.7 copy.46
  160.4 0.4 convolution_add_fusion.2
  160.9 37.0 %all-reduce.2 = (f32[32]{0:T(128)S(1)}, f32[32]{0:T(128)S(1)}, f32[32]{0:T(128)S(1)}, f32[32,8]{0,1:T(8,128)S(1)}) all-reduce(f32[32]{0:T(128)S(1)} %get-tuple-element.52, f32[32]{0:T(128)S(1)} %broadcast_multiply_fusion.2, f32[32]{0:T(128)S(1)} %get-tuple-element.48, ...), channel_id=1, replica_groups=mesh['row'=4,'col'=2,'win'=4] {'row','col','win'}, use_global_device_ids=true, to_apply=%region_13.0 | all-reduce | flops 352 | bytes 2816 | tf_op jit(solution)/shard_map/psum | solution.py:65
  197.9 1.0 copy.48
  199.0 0.8 copy.47
  200.0 10.0 %all_gather.29 = f32[32,128]{0,1:T(8,128)S(1)} all-gather(f32[32,16]{0,1:T(8,128)S(1)} %copy.28), channel_id=1, replica_groups=mesh['row'=4,'col'=2,'win'=4] {'col','win'}, dimensions={1}, use_global_device_ids=true | all-gather | bytes 18432 | tf_op jit(solution)/shard_map/all_gather | solution.py:13
  210.1 46.2 %reduce-scatter.31.cloned.1.call-done = f32[64,32]{1,0:T(8,128)} async-done(((f32[1024,32]{1,0:T(8,128)}), f32[64,32]{1,0:T(8,128)}) %reduce-scatter.31.cloned.1.call-update) | async-done | bytes 8208
  256.3 0.8 copy.49
  257.3 20.3 %all-gather.2 = f32[16,64,32]{1,2,0:T(8,128)S(1)} all-gather(f32[1,64,32]{1,2,0:T(8,128)S(1)} %bitcast.122), channel_id=1, replica_groups=mesh['row'=4,'col'=2,'win'=4] {'row','win'}, dimensions={0}, use_global_device_ids=true | all-gather | bytes 139264 | tf_op jit(solution)/shard_map/all_gather | solution.py:14
  277.9 0.7 convolution_divide_fusion.2
  278.6 0.6 fusion.58
  279.2 0.7 convolution_divide_fusion.3
  279.9 0.4 fusion.7
  280.3 0.7 multiply_reduce_fusion.3
  281.1 0.7 copy.50
  281.9 0.4 convolution_add_fusion.1
  282.3 37.0 %all-reduce.1 = (f32[32]{0:T(128)S(1)}, f32[32]{0:T(128)S(1)}, f32[32]{0:T(128)S(1)}, f32[32,8]{0,1:T(8,128)S(1)}) all-reduce(f32[32]{0:T(128)S(1)} %get-tuple-element.46, f32[32]{0:T(128)S(1)} %broadcast_multiply_fusion.1, f32[32]{0:T(128)S(1)} %get-tuple-element.42, ...), channel_id=1, replica_groups=mesh['row'=4,'col'=2,'win'=4] {'row','col','win'}, use_global_device_ids=true, to_apply=%region_24.0 | all-reduce | flops 352 | bytes 2816 | tf_op jit(solution)/shard_map/psum | solution.py:65
  319.3 1.0 copy.52
  320.4 0.8 copy.51
  321.5 10.0 %all_gather.31 = f32[32,128]{0,1:T(8,128)S(1)} all-gather(f32[32,16]{0,1:T(8,128)S(1)} %copy.34), channel_id=1, replica_groups=mesh['row'=4,'col'=2,'win'=4] {'col','win'}, dimensions={1}, use_global_device_ids=true | all-gather | bytes 18432 | tf_op jit(solution)/shard_map/all_gather | solution.py:13
  331.5 46.2 %reduce-scatter.35.cloned.1.call-done = f32[64,32]{1,0:T(8,128)} async-done(((f32[1024,32]{1,0:T(8,128)}), f32[64,32]{1,0:T(8,128)}) %reduce-scatter.35.cloned.1.call-update) | async-done | bytes 8208
  377.7 0.8 copy.53
  378.5 0.2 fusion.46
  378.7 20.2 %all-gather.3 = f32[16,64,32]{1,2,0:T(8,128)S(1)} all-gather(f32[1,64,32]{1,2,0:T(8,128)S(1)} %bitcast.124), channel_id=1, replica_groups=mesh['row'=4,'col'=2,'win'=4] {'row','win'}, dimensions={0}, use_global_device_ids=true | all-gather | bytes 139264 | tf_op jit(solution)/shard_map/all_gather | solution.py:14
  399.2 0.7 convolution_divide_fusion
  399.9 0.6 fusion.59
  400.6 0.7 convolution_divide_fusion.1
  401.3 0.4 fusion.2
  401.7 0.7 multiply_reduce_fusion.1
  402.4 0.7 copy.54
  403.2 0.4 convolution_add_fusion
  403.6 1.0 copy.56
  404.7 37.0 %all-reduce = (f32[32]{0:T(128)S(1)}, f32[32]{0:T(128)S(1)}, f32[32]{0:T(128)S(1)}, f32[32,8]{0,1:T(8,128)S(1)}) all-reduce(f32[32]{0:T(128)S(1)} %get-tuple-element.40, f32[32]{0:T(128)S(1)} %broadcast_multiply_fusion, f32[32]{0:T(128)S(1)} %get-tuple-element.36, ...), channel_id=1, replica_groups=mesh['row'=4,'col'=2,'win'=4] {'row','col','win'}, use_global_device_ids=true, to_apply=%region_35.0 | all-reduce | flops 352 | bytes 2816 | tf_op jit(solution)/shard_map/psum | solution.py:65
  441.7 0.6 add_multiply_fusion.8
  442.2 0.8 copy.55
  443.1 0.7 copy.41
  443.8 49.8 %reduce-scatter.39.cloned.1.call-done = f32[64,32]{1,0:T(8,128)} async-done(((f32[1024,32]{1,0:T(8,128)}), f32[64,32]{1,0:T(8,128)}) %reduce-scatter.39.cloned.1.call-update) | async-done | bytes 8208
  493.6 0.8 copy.57
  494.4 0.7 add_multiply_fusion
  (76 shorter events, 3.4 us)
Async XLA Ops:
  7.2 78.0 %reduce-scatter.25.cloned.1.call-start = ((), (), s32[]{:S(2)}) async-start(), calls=%async_computation.8 | async-start | bytes 73728
  18.0 0.7 copy-start
  18.0 23.7 %copy-start.3 = (s32[2,128,1024]{2,1,0:T(8,128)S(1)}, s32[2,128,1024]{2,1,0:T(8,128)}, u32[]{:S(2)}) copy-start(s32[2,128,1024]{2,1,0:T(8,128)} %param.4) | copy-start | bytes 3145732
  41.1 0.7 copy-start.2
  45.3 89.6 %reduce-scatter.27.cloned.1.call-start = ((), (), s32[]{:S(2)}) async-start(), calls=%async_computation.9 | async-start | bytes 557056
  47.2 151.8 %reduce-scatter.29.cloned.1.call-start = ((), (), s32[]{:S(2)}) async-start(), calls=%async_computation.10 | async-start | bytes 73728
  47.4 0.7 copy-start.1
  160.4 95.9 %reduce-scatter.31.cloned.1.call-start = ((), (), s32[]{:S(2)}) async-start(), calls=%async_computation.11 | async-start | bytes 557056
  198.9 121.5 %reduce-scatter.33.cloned.1.call-start = ((), (), s32[]{:S(2)}) async-start(), calls=%async_computation.12 | async-start | bytes 73728
  281.8 95.9 %reduce-scatter.35.cloned.1.call-start = ((), (), s32[]{:S(2)}) async-start(), calls=%async_computation.13 | async-start | bytes 557056
  320.4 121.9 %reduce-scatter.37.cloned.1.call-start = ((), (), s32[]{:S(2)}) async-start(), calls=%async_computation.14 | async-start | bytes 73728
  403.2 90.4 %reduce-scatter.39.cloned.1.call-start = ((), (), s32[]{:S(2)}) async-start(), calls=%async_computation.15 | async-start | bytes 557056
Sparse Core Ops, SparseCore 0:
  45.4 29.7 reduce-scatter.24
  79.2 55.7 reduce-scatter.26
  160.5 30.4 reduce-scatter.28
  199.0 57.1 reduce-scatter.30
  282.0 30.4 reduce-scatter.32
  320.5 57.1 reduce-scatter.34
  403.3 30.4 reduce-scatter.36
  437.7 55.7 reduce-scatter.38
where the time goes:
time: 503 us; the launch traced here: 502 us
  blocking collectives  271 us (54%)
  waiting for transfers between devices  181 us (36%)
  local copies, waits for them, and re-layouts  17.5 us (3%)
  between operations  14.5 us (3%)
  matrix products  14.3 us (3%)
    unnamed x16, waiting for transfers between devices  181 us
    psum x4, blocking collectives, local(): lax.psum((jnp.sum(row_shard, axis=1), jnp.sum(col_shard, axis=1), jnp.sum...  148 us
    all_gather x4, blocking collectives, fetch_blocks(): col_block = lax.all_gather(col_shard, ('row', 'win'), axis=1, tiled=True)  82.8 us
    all_gather x4, blocking collectives, fetch_blocks(): row_block = lax.all_gather(row_shard, ('col', 'win'), axis=1, tiled=True)  40.9 us
    unnamed x30, local copies, waits for them, and re-layouts  16.4 us
  transfers between devices with their start and end apart: 8, of which 4 were waited for; matrix products, arithmetic and copies ran while one was open for 2% of the time, Pallas kernels for 0%

commit v1 on v0

v1 whole, which is shorter than its diff:
```python
import functools

import jax
import jax.numpy as jnp
from jax import lax
from jax.experimental import pallas as pl
from jax.experimental.pallas import tpu as pltpu
from jax.sharding import PartitionSpec as P

STEPS = 4
LANES = 128
MESH = pl.DeviceIdType.MESH
F32 = jnp.float32
BF16 = jnp.bfloat16


def dot(a, b):
    return lax.dot_general(a, b, (((1,), (0,)), ((), ())), preferred_element_type=F32)


def split(value):
    high = value.astype(BF16)
    low = (value - high.astype(F32)).astype(BF16)
    return high, low


def kernel(
    sizes,
    counts_ref, row_ref, col_ref, win_ref,
    row_out, col_out, win_out,
    cnt, cnt_send, a_now, b_now, c_now, scale_a, pa_now,
    ia, ib, pa_send, rr, pb_send, rc, ga, gb, zs,
    sems,
):
    nrow, ncol, nwin = sizes
    rank, row_width = row_ref.shape
    col_width = col_ref.shape[1]
    own_wins, items, columns = counts_ref.shape
    half = columns // 2
    nx = nwin // 2
    npr, npc = ncol * nwin, nrow * nx
    groups = half // LANES
    rk_r, rk_c = rank // npr, rank * groups // npc
    local_wins = 2 * own_wins

    row, col, win = lax.axis_index("row"), lax.axis_index("col"), lax.axis_index("win")
    xpos, core = win // 2, win % 2
    me_r = col * nwin + win
    me_c = row * nx + xpos

    def row_peer(d):
        q = (me_r + d) % npr
        return q, (row, q // nwin, q % nwin)

    def col_peer(d):
        q = (me_c + d) % npc
        return q, (q // nx, col, (q % nx) * 2 + core)

    def z_peer(d):
        q = (row + d) % nrow
        return q, (q, col, win)

    def remote(src, dst, kind, device):
        return pltpu.make_async_remote_copy(
            src_ref=src, dst_ref=dst, send_sem=sems.at[0, kind], recv_sem=sems.at[1, kind],
            device_id=device, device_id_type=MESH,
        )

    def wait_all(slots, kind, device):
        n = slots.shape[0] - 1
        part = slots.at[pl.ds(0, n)]
        both = remote(part, part, kind, device)
        both.wait_recv()

    def wait_sent(slots, kind, device):
        n = slots.shape[0] - 1
        part = slots.at[pl.ds(0, n)]
        remote(part, part, kind, device).wait_send()

    some_row, some_col, some_z = row_peer(1)[1], col_peer(1)[1], z_peer(1)[1]
    partner = (row, col, 2 * xpos + (1 - core))

    barrier = pltpu.get_barrier_semaphore()
    for d in range(1, npr):
        pl.semaphore_signal(barrier, inc=1, device_id=row_peer(d)[1], device_id_type=MESH)
    for d in range(1, npc):
        pl.semaphore_signal(barrier, inc=1, device_id=col_peer(d)[1], device_id_type=MESH)

    ia[me_r] = jnp.zeros((rank, LANES), F32)
    ia[me_r, :, 0:row_width] = row_ref[...]
    ia[me_r, :, row_width : row_width + own_wins] = win_ref[...]
    ib[me_c] = jnp.zeros((rank, LANES), F32)
    ib[me_c, :, 0:col_width] = col_ref[...]

    pl.semaphore_wait(barrier, npr - 1 + npc - 1)

    for d in range(1, npc):
        remote(ib.at[me_c], ib.at[me_c], 0, col_peer(d)[1]).start()
    for d in range(1, npr):
        remote(ia.at[me_r], ia.at[me_r], 1, row_peer(d)[1]).start()

    span = 2 * LANES
    src_at = lax.broadcasted_iota(jnp.int32, (span, span), 0)
    dst_at = lax.broadcasted_iota(jnp.int32, (span, span), 1)
    side = dst_at // LANES
    lane = dst_at % LANES
    take = jnp.where(side == 0, core, 1 - core)
    origin = (lane // col_width) * (2 * col_width) + take * col_width + lane % col_width
    order = jnp.where(src_at == origin, 1.0, 0.0).astype(BF16)
    base = core * (own_wins * items)
    for w in range(own_wins):
        for g in range(groups):
            block = counts_ref[w, :, g * span : (g + 1) * span].astype(F32).astype(BF16)
            moved = dot(block, order)
            at = pl.ds(pl.multiple_of(base + w * items, items), items)
            cnt[at, g * LANES : (g + 1) * LANES] = moved[:, :LANES]
            cnt_send[w * items : (w + 1) * items, g * LANES : (g + 1) * LANES] = moved[:, LANES:]
    mine = cnt.at[pl.ds(pl.multiple_of(base, items), own_wins * items)]
    swap = remote(cnt_send, mine, 2, partner)
    swap.start()

    lane_at = lax.broadcasted_iota(jnp.int32, (rank, LANES), 1)
    row_at = lax.broadcasted_iota(jnp.int32, (LANES, LANES), 0)

    wait_all(ib, 0, some_col)
    per = LANES // col_width
    for g in range(groups):
        block = ib[g * per]
        for m in range(1, per):
            moved = pltpu.roll(ib[g * per + m], m * col_width, 1)
            block = jnp.where(lane_at // col_width == m, moved, block)
        b_now[:, g * LANES : (g + 1) * LANES] = block
    wait_all(ia, 1, some_row)
    block = ia[0]
    for m in range(1, npr):
        moved = pltpu.roll(ia[m], m * row_width, 1)
        block = jnp.where(lane_at // row_width == m, moved, block)
    a_now[...] = block
    wins = jnp.zeros((rank, LANES), F32)
    for w in range(nwin):
        moved = pltpu.roll(ia[w], (LANES - row_width + w * own_wins) % LANES, 1)
        wins = jnp.where(lane_at // own_wins == w, moved, wins)
    pad = jnp.zeros((LANES - rank, LANES), F32)
    c_now[...] = jnp.transpose(jnp.concatenate([wins, pad], axis=0))[: nwin * own_wins]
    wait_sent(ib, 0, some_col)
    wait_sent(ia, 1, some_row)
    swap.wait()

    def local_c():
        rows = c_now[0:local_wins, :]
        for g in range(1, nx):
            rows = jnp.where(xpos == g, c_now[g * local_wins : (g + 1) * local_wins, :], rows)
        return rows

    def step(_, carry):
        a = a_now[...]
        b = b_now[...]
        rows = jnp.concatenate([local_c(), jnp.zeros((LANES - local_wins, LANES), F32)], axis=0)
        cols = jnp.transpose(rows)[:rank]
        weights = [jnp.broadcast_to(cols[:, w : w + 1], (rank, items)) for w in range(local_wins)]
        scaled = jnp.concatenate([a * weight for weight in weights], axis=1)
        s_high, s_low = split(scaled)
        b_high, b_low = split(b)
        sh, sl = s_high.astype(F32), s_low.astype(F32)
        left = jnp.transpose(jnp.concatenate([sh, sh, sl, sl], axis=0)).astype(BF16)
        right = jnp.concatenate([b_high, b_low, b_high, b_low], axis=0)
        model = dot(left, right)
        ratio = cnt[...] / model
        r_high, r_low = split(ratio)

        both = dot(jnp.concatenate([s_high, s_low], axis=0), r_high)
        pb = both[:rank] + both[rank:] + dot(s_high, r_low)
        for q in range(npc):
            g, top = q % groups, (q // groups) * rk_c
            pb_send[q] = pb[top : top + rk_c, g * LANES : (g + 1) * LANES]
        for d in range(1, npc):
            q, device = col_peer(d)
            remote(pb_send.at[q], rc.at[me_c], 3, device).start()
        rc[me_c] = pb_send[me_c]

        bt = jnp.transpose(jnp.concatenate([b_high.astype(F32), b_low.astype(F32)], axis=0))
        bt = bt.astype(BF16)
        back = jnp.transpose(dot(r_high, bt) + dot(r_low, bt))
        back = back[:rank] + back[rank:]
        pa = jnp.zeros((rank, items), F32)
        stats = jnp.zeros((rank, LANES), F32)
        for w in range(local_wins):
            part = back[:, w * items : (w + 1) * items]
            pa = pa + part * weights[w]
            stats = jnp.where(lane_at == w, jnp.sum(part * a, axis=1, keepdims=True), stats)
        stats = jnp.where(lane_at == local_wins, jnp.sum(b, axis=1, keepdims=True), stats)
        stats = jnp.where(lane_at == local_wins + 1, jnp.sum(a, axis=1, keepdims=True), stats)
        stat_rows = jnp.transpose(jnp.concatenate([stats, pad], axis=0))[:8]
        pa_now[...] = pa
        for q in range(npr):
            pa_send[q, 0:8] = stat_rows
            pa_send[q, 8 : 8 + rk_r] = pa_now[q * rk_r : (q + 1) * rk_r, :]
        for d in range(1, npr):
            q, device = row_peer(d)
            remote(pa_send.at[q], rr.at[me_r], 4, device).start()
        rr[me_r] = pa_send[me_r]

        wait_all(rr, 4, some_row)
        total = rr[0, 8 : 8 + rk_r]
        for q in range(1, npr):
            total = total + rr[q, 8 : 8 + rk_r]
        ga[me_r] = total
        for g in range(nx):
            parts = [rr[c * nwin + 2 * g + k, 0:8] for c in range(ncol) for k in range(2)]
            zs[row, g * 8 : (g + 1) * 8] = functools.reduce(jnp.add, parts)
        for d in range(1, npr):
            remote(ga.at[me_r], ga.at[me_r], 5, row_peer(d)[1]).start()

        wait_all(rc, 3, some_col)
        for d in range(1, nrow):
            remote(zs.at[row], zs.at[row], 6, z_peer(d)[1]).start()
        total = rc[0]
        for q in range(1, npc):
            total = total + rc[q]
        gb[me_c] = total
        for d in range(1, npc):
            remote(gb.at[me_c], gb.at[me_c], 7, col_peer(d)[1]).start()

        wait_all(zs, 6, some_z)
        stat = zs[0]
        for q in range(1, nrow):
            stat = stat + zs[q]
        sum_b = stat[local_wins : local_wins + 1] * (1.0 / nrow)
        sum_a = stat[local_wins + 1 : local_wins + 2] * (1.0 / (2 * ncol))
        wins_now = c_now[...]
        sum_c = jnp.sum(wins_now, axis=0, keepdims=True)
        for g in range(nx):
            old = c_now[g * local_wins : (g + 1) * local_wins, :]
            terms = old * stat[g * 8 : g * 8 + local_wins]
            valid = lax.broadcasted_iota(jnp.int32, (local_wins, LANES), 1) < rank
            c_now[g * local_wins : (g + 1) * local_wins, :] = jnp.where(
                valid, old * (0.5 + 0.5 * terms / (sum_a * sum_b)), 0.0
            )
        norm_a = 0.5 / (sum_b * sum_c)
        norm_b = 0.5 / (sum_a * sum_c)
        norms = jnp.where(row_at == 0, norm_a, jnp.where(row_at == 1, norm_b, 0.0))
        norms = jnp.transpose(norms)[:rank]
        scale_a[...] = jnp.broadcast_to(norms[:, 0:1], (rank, items))
        wait_all(ga, 5, some_row)
        for q in range(npr):
            at = slice(q * rk_r, (q + 1) * rk_r)
            a_now[at, :] = a_now[at, :] * (0.5 + scale_a[at, :] * ga[q])
        scale_a[...] = jnp.broadcast_to(norms[:, 1:2], (rank, items))
        wait_all(gb, 7, some_col)
        for q in range(npc):
            g, top = q % groups, (q // groups) * rk_c
            at, over = slice(top, top + rk_c), slice(g * LANES, (g + 1) * LANES)
            b_now[at, over] = b_now[at, over] * (0.5 + scale_a[at, :] * gb[q])

        wait_sent(pb_send, 3, some_col)
        wait_sent(pa_send, 4, some_row)
        wait_sent(ga, 5, some_row)
        wait_sent(zs, 6, some_z)
        wait_sent(gb, 7, some_col)
        return carry

    lax.fori_loop(0, STEPS, step, 0)

    shift = (LANES - me_r * row_width) % LANES
    row_out[...] = pltpu.roll(a_now[...], shift, 1)[:, :row_width]
    block = b_now[:, 0:LANES]
    for g in range(1, groups):
        block = jnp.where(me_c // per == g, b_now[:, g * LANES : (g + 1) * LANES], block)
    shift = (LANES - (me_c % per) * col_width) % LANES
    col_out[...] = pltpu.roll(block, shift, 1)[:, :col_width]
    all_wins = nwin * own_wins
    rows = jnp.concatenate([c_now[...], jnp.zeros((LANES - all_wins, LANES), F32)], axis=0)
    cols = jnp.transpose(rows)[:rank]
    win_out[...] = pltpu.roll(cols, (LANES - win * own_wins) % LANES, 1)[:, :own_wins]


def local(sizes, counts, rows, cols, wins):
    nrow, ncol, nwin = sizes
    rank, row_width = rows.shape
    own_wins, items, columns = counts.shape
    half = columns // 2
    nx = nwin // 2
    npr, npc = ncol * nwin, nrow * nx
    rk_r, rk_c = rank // npr, rank * (half // LANES) // npc
    vmem = lambda *shape: pltpu.VMEM(shape, F32)
    spec = pl.BlockSpec(memory_space=pltpu.VMEM)
    return pl.pallas_call(
        functools.partial(kernel, sizes),
        out_shape=[jax.ShapeDtypeStruct(v.shape, F32) for v in (rows, cols, wins)],
        in_specs=[spec] * 4,
        out_specs=[spec] * 3,
        scratch_shapes=[
            vmem(2 * own_wins * items, half),
            vmem(own_wins * items, half),
            vmem(rank, items),
            vmem(rank, half),
            vmem(nwin * own_wins, LANES),
            vmem(rank, items),
            vmem(rank, items),
            vmem(npr, rank, LANES),
            vmem(npc, rank, LANES),
            vmem(npr, 8 + rk_r, LANES),
            vmem(npr, 8 + rk_r, LANES),
            vmem(npc, rk_c, LANES),
            vmem(npc, rk_c, LANES),
            vmem(npr, rk_r, LANES),
            vmem(npc, rk_c, LANES),
            vmem(nrow, 8 * nx, LANES),
            pltpu.SemaphoreType.DMA((2, 8)),
        ],
        compiler_params=pltpu.CompilerParams(
            collective_id=0, has_side_effects=True, vmem_limit_bytes=40 * 1024 * 1024
        ),
    )(counts, rows, cols, wins)


def solution(mesh):
    in_specs = (
        P("win", "row", "col"),
        P(None, ("row", "col", "win")),
        P(None, ("col", "row", "win")),
        P(None, "win"),
    )
    out_specs = (P(None, ("row", "col", "win")), P(None, ("col", "row", "win")), P(None, "win"))
    sizes = (mesh.shape["row"], mesh.shape["col"], mesh.shape["win"])
    return jax.shard_map(
        functools.partial(local, sizes), mesh=mesh, in_specs=in_specs, out_specs=out_specs, check_vma=False
    )
```

time: 503 us -> 55 us (0.11)
  blocking collectives: 271 us -> 0 us
  waiting for transfers between devices: 181 us -> 0 us
  Pallas kernels: 0 us -> 50.1 us
  matrix products: 14.3 us -> 0 us
  between operations: 14.5 us -> 0.66 us
  local copies, waits for them, and re-layouts: 17.5 us -> 4.01 us
    unnamed x16 -> x0, waiting for transfers between devices: 181 us -> none
    psum x4 -> x0, blocking collectives: 148 us -> none  [local(): lax.psum((jnp.sum(row_shard, axis=1), jnp.sum(col_shard, axis=1), jnp.sum...]
    all_gather x8 -> x0, blocking collectives: 124 us -> none  [the longest x4 82.8 us: fetch_blocks(): col_block = lax.all_gather(col_shard, ('row', 'win'), axis=1, tiled=True)]
    pallas_call x0 -> x1, Pallas kernels: none -> 50.1 us  [local(): pl.pallas_call(functools.partial(kernel, sizes), out_shape=[jax.ShapeDtyp...]
    dot_general x24 -> x0, matrix products: 14.3 us -> none  [the longest x8 5.84 us: block_terms(): lax.dot_general(scaled, col_block, (((0,), (0,)), ((), ())), precision=HI...]
    unnamed x30 -> x9, local copies, waits for them, and re-layouts: 16.4 us -> 2.71 us
  transfers between devices with their start and end apart: 8 -> 0, of which waited for: 4 -> 0; matrix products, arithmetic and copies ran while one was open for 2% -> 0% of each run, Pallas kernels for 0% -> 0%
where the time goes in v1:
time: 55 us; the launch traced here: 54.8 us
  Pallas kernels  50.1 us (91%)
  local copies, waits for them, and re-layouts  4.01 us (7%)
  between operations  0.66 us (1%)
    pallas_call x1, Pallas kernels, local(): pl.pallas_call(functools.partial(kernel, sizes), out_shape=[jax.ShapeDtyp...  50.1 us
    unnamed x9, local copies, waits for them, and re-layouts  2.71 us
    pallas_call x2, local copies, waits for them, and re-layouts, local(): pl.pallas_call(functools.partial(kernel, sizes), out_shape=[jax.ShapeDtyp...  1.3 us

profile of v1, /device:TPU:0, one launch (start us, length us, event | category | flops | bytes accessed | tf_op | source)
XLA Modules:
  0.0 54.8 jit_solution(11492117332647778422)
XLA Ops:
  0.6 0.0 copy-start.2
  0.6 0.0 copy-start.1
  0.7 0.8 %copy.7.row_ref = f32[32,16]{1,0:T(8,128)S(1)} copy(f32[32,16]{0,1:T(8,128)} %param.5) | data formatting | bytes 4096 | tf_op args[1]
  1.4 0.0 copy-done.2
  1.4 0.1 copy.8.win_ref
  1.5 0.0 copy-done.1
  1.5 0.0 copy-start
  1.5 1.2 %copy-done = s32[2,128,1024]{2,1,0:T(8,128)S(1)} copy-done((s32[2,128,1024]{2,1,0:T(8,128)S(1)}, s32[2,128,1024]{2,1,0:T(8,128)}, u32[]{:S(2)}) %copy-start) | copy-done | bytes 1048600
  2.8 50.1 %shard_map.67 = (f32[32,16]{1,0:T(8,128)S(1)}, f32[32,64]{1,0:T(8,128)S(1)}, f32[32,2]{1,0:T(8,128)S(1)}) custom-call(s32[2,128,1024]{2,1,0:T(8,128)S(1)} %copy-done, f32[32,16]{1,0:T(8,128)S(1)} %copy.7.row_ref, f32[32,64]{1,0:T(8,128)S(1)} %copy-done.1, f32[32,2]{1,0:T(8,128)S(1)} %copy.8.win_ref), custom_call_target="tpu_custom_call" | custom-call | tf_op jit(solution)/shard_map/pallas_call | solution.py:287
  52.9 0.7 %copy.9 = f32[32,16]{0,1:T(8,128)} copy(f32[32,16]{1,0:T(8,128)S(1)} %get-tuple-element.3) | data formatting | bytes 4096 | tf_op jit(solution)/shard_map/pallas_call | solution.py:287
  53.5 0.6 %copy.10 = f32[32,2]{0,1:T(2,128)} copy(f32[32,2]{1,0:T(8,128)S(1)} %get-tuple-element.5) | data formatting | bytes 512 | tf_op jit(solution)/shard_map/pallas_call | solution.py:287
  54.2 0.6 %copy.12 = f32[32,64]{1,0:T(8,128)} copy(f32[32,64]{1,0:T(8,128)S(1)} %get-tuple-element.10) | data formatting | bytes 16384
Async XLA Ops:
  0.6 0.8 %copy-start.2 = (f32[32,2]{0,1:T(2,128)S(1)}, f32[32,2]{0,1:T(2,128)}, u32[]{:S(2)}) copy-start(f32[32,2]{0,1:T(2,128)} %param.7) | copy-start | bytes 772
  0.6 0.9 %copy-start.1 = (f32[32,64]{1,0:T(8,128)S(1)}, f32[32,64]{1,0:T(8,128)}, u32[]{:S(2)}) copy-start(f32[32,64]{1,0:T(8,128)} %col_ref.1) | copy-start | bytes 24580
  1.5 1.2 %copy-start = (s32[2,128,1024]{2,1,0:T(8,128)S(1)}, s32[2,128,1024]{2,1,0:T(8,128)}, u32[]{:S(2)}) copy-start(s32[2,128,1024]{2,1,0:T(8,128)} %counts_ref.1) | copy-start | bytes 3145732

commit v2 on v1

v2 whole, which is shorter than its diff:
```python
import functools

import jax
import jax.numpy as jnp
from jax import lax
from jax.experimental import pallas as pl
from jax.experimental.pallas import tpu as pltpu
from jax.sharding import PartitionSpec as P

STEPS = 4
LANES = 128
MESH = pl.DeviceIdType.MESH
F32 = jnp.float32
BF16 = jnp.bfloat16


def dot(a, b):
    return lax.dot_general(a, b, (((1,), (0,)), ((), ())), preferred_element_type=F32)


def split(value):
    high = value.astype(BF16)
    low = (value - high.astype(F32)).astype(BF16)
    return high, low


def kernel(
    sizes,
    counts_ref, row_ref, col_ref, win_ref,
    row_out, col_out, win_out,
    counts_here, cnt, cnt_send, a_now, b_now, c_now, cols_now, left_now, high_now, low_now, tile,
    ia, ib, rr, pb_send, rc, gb, zs,
    sems, load_sem,
):
    nrow, ncol, nwin = sizes
    row_width, rank = row_ref.shape
    col_width = col_ref.shape[1]
    own_wins, items, columns = counts_ref.shape
    half = columns // 2
    nx = nwin // 2
    npr, npc = ncol * nwin, nrow * nx
    groups = half // LANES
    first_row, owner_rows = nrow // 4, nrow // 2
    npo = owner_rows * nx
    rk_c = rank * groups // npo
    local_wins = 2 * own_wins

    row, col, win = lax.axis_index("row"), lax.axis_index("col"), lax.axis_index("win")
    xpos, core = win // 2, win % 2
    me_r = col * nwin + win
    me_c = row * nx + xpos
    me_o = me_c - first_row * nx
    is_owner = jnp.logical_and(me_o >= 0, me_o < npo)
    not_owner = jnp.logical_not(is_owner)

    def row_peer(d):
        q = (me_r + d) % npr
        return q, (row, q // nwin, q % nwin)

    def col_peer(d):
        q = (me_c + d) % npc
        return q, (q // nx, col, (q % nx) * 2 + core)

    def z_peer(d):
        q = (row + d) % nrow
        return q, (q, col, win)

    def remote(src, dst, kind, device):
        return pltpu.make_async_remote_copy(
            src_ref=src, dst_ref=dst, send_sem=sems.at[0, kind], recv_sem=sems.at[1, kind],
            device_id=device, device_id_type=MESH,
        )

    def wait_all(slots, kind, device, n=None):
        part = slots.at[pl.ds(0, slots.shape[0] - 1 if n is None else n)]
        remote(part, part, kind, device).wait_recv()

    def wait_sent(slots, kind, device, n=None):
        part = slots.at[pl.ds(0, slots.shape[0] - 1 if n is None else n)]
        remote(part, part, kind, device).wait_send()

    some_row, some_col, some_z = row_peer(1)[1], col_peer(1)[1], z_peer(1)[1]
    partner = (row, col, 2 * xpos + (1 - core))

    barrier = pltpu.get_barrier_semaphore()
    for d in range(1, npr):
        pl.semaphore_signal(barrier, inc=1, device_id=row_peer(d)[1], device_id_type=MESH)
    for d in range(1, npc):
        pl.semaphore_signal(barrier, inc=1, device_id=col_peer(d)[1], device_id_type=MESH)

    load = pltpu.make_async_copy(counts_ref, counts_here, load_sem)
    load.start()
    tile[...] = jnp.zeros((LANES, LANES), F32)
    tile[0:row_width, 0:rank] = row_ref[...]
    tile[row_width : row_width + own_wins, 0:rank] = win_ref[...]
    ia[me_r] = jnp.transpose(tile[...])[:rank]
    ib[me_c] = jnp.zeros((rank, LANES), F32)
    ib[me_c, :, 0:col_width] = col_ref[...]

    pl.semaphore_wait(barrier, npr - 1 + npc - 1)

    for d in range(1, npc):
        remote(ib.at[me_c], ib.at[me_c], 0, col_peer(d)[1]).start()
    for d in range(1, npr):
        remote(ia.at[me_r], ia.at[me_r], 1, row_peer(d)[1]).start()

    span = 2 * LANES
    src_at = lax.broadcasted_iota(jnp.int32, (span, span), 0)
    dst_at = lax.broadcasted_iota(jnp.int32, (span, span), 1)
    side = dst_at // LANES
    lane = dst_at % LANES
    take = jnp.where(side == 0, core, 1 - core)
    origin = (lane // col_width) * (2 * col_width) + take * col_width + lane % col_width
    order = jnp.where(src_at == origin, 1.0, 0.0).astype(BF16)
    base = core * (own_wins * items)
    load.wait()
    for w in range(own_wins):
        for g in range(groups):
            block = counts_here[w, :, g * span : (g + 1) * span].astype(F32).astype(BF16)
            moved = dot(block, order)
            at = pl.ds(pl.multiple_of(base + w * items, items), items)
            cnt[at, g * LANES : (g + 1) * LANES] = moved[:, :LANES]
            cnt_send[w * items : (w + 1) * items, g * LANES : (g + 1) * LANES] = moved[:, LANES:]
    mine = cnt.at[pl.ds(pl.multiple_of(base, items), own_wins * items)]
    swap = remote(cnt_send, mine, 8, partner)
    swap.start()

    lane_at = lax.broadcasted_iota(jnp.int32, (rank, LANES), 1)
    row_at = lax.broadcasted_iota(jnp.int32, (LANES, LANES), 0)

    wait_all(ib, 0, some_col)
    per = LANES // col_width
    for g in range(groups):
        block = ib[g * per]
        for m in range(1, per):
            moved = pltpu.roll(ib[g * per + m], m * col_width, 1)
            block = jnp.where(lane_at // col_width == m, moved, block)
        b_now[:, g * LANES : (g + 1) * LANES] = block
    wait_all(ia, 1, some_row)
    block = ia[0]
    for m in range(1, npr):
        moved = pltpu.roll(ia[m], m * row_width, 1)
        block = jnp.where(lane_at // row_width == m, moved, block)
    a_now[...] = block
    wins = jnp.zeros((rank, LANES), F32)
    for w in range(nwin):
        moved = pltpu.roll(ia[w], (LANES - row_width + w * own_wins) % LANES, 1)
        wins = jnp.where(lane_at // own_wins == w, moved, wins)
    pad = jnp.zeros((LANES - rank, LANES), F32)
    c_now[...] = jnp.transpose(jnp.concatenate([wins, pad], axis=0))[: nwin * own_wins]
    wait_sent(ib, 0, some_col)
    wait_sent(ia, 1, some_row)
    swap.wait()

    def local_c():
        rows = c_now[0:local_wins, :]
        for g in range(1, nx):
            rows = jnp.where(xpos == g, c_now[g * local_wins : (g + 1) * local_wins, :], rows)
        return rows

    def put_cols(extra):
        rows = jnp.concatenate([local_c(), jnp.zeros((LANES - local_wins, LANES), F32)], axis=0)
        rows = jnp.where(row_at == local_wins, extra, rows)
        cols_now[...] = jnp.transpose(rows)[:rank]

    def weight(w):
        return jnp.broadcast_to(cols_now[:, w : w + 1], (rank, items))

    def prepare():
        a = a_now[...]
        scaled = jnp.concatenate([a * weight(w) for w in range(local_wins)], axis=1)
        s_high, s_low = split(scaled)
        sh, sl = s_high.astype(F32), s_low.astype(F32)
        left_now[...] = jnp.transpose(jnp.concatenate([sh, sh, sl, sl], axis=0)).astype(BF16)
        high_now[...] = s_high
        low_now[...] = s_low

    def step(index, carry):
        odd = index % 2
        k_rr, k_zs = 4 + odd, 6 + odd
        b = b_now[...]
        b_high, b_low = split(b)
        right = jnp.concatenate([b_high, b_low, b_high, b_low], axis=0)
        ratio = cnt[...] / dot(left_now[...], right)
        r_high, r_low = split(ratio)

        s_high = high_now[...]
        both = dot(jnp.concatenate([s_high, low_now[...]], axis=0), r_high)
        pb = both[:rank] + both[rank:] + dot(s_high, r_low)
        for o in range(npo):
            g, top = o % groups, (o // groups) * rk_c
            pb_send[o] = pb[top : top + rk_c, g * LANES : (g + 1) * LANES]
        for o in range(npo):

            @pl.when(me_o != o)
            def _(o=o):
                device = (first_row + o // nx, col, (o % nx) * 2 + core)
                remote(pb_send.at[o], rc.at[me_c], 3, device).start()

        a = a_now[...]
        bt = jnp.transpose(jnp.concatenate([b_high.astype(F32), b_low.astype(F32)], axis=0))
        bt = bt.astype(BF16)
        back = jnp.transpose(dot(r_high, bt) + dot(r_low, bt))
        back = back[:rank] + back[rank:]
        pa = jnp.zeros((rank, items), F32)
        stats = jnp.zeros((rank, LANES), F32)
        for w in range(local_wins):
            part = back[:, w * items : (w + 1) * items]
            pa = pa + part * weight(w)
            stats = jnp.where(lane_at == w, jnp.sum(part * a, axis=1, keepdims=True), stats)
        stats = jnp.where(lane_at == local_wins, jnp.sum(b, axis=1, keepdims=True), stats)
        stats = jnp.where(lane_at == local_wins + 1, jnp.sum(a, axis=1, keepdims=True), stats)
        rr[odd, me_r, 0:rank] = pa
        rr[odd, me_r, rank : rank + 8] = jnp.transpose(jnp.concatenate([stats, pad], axis=0))[:8]
        for d in range(1, npr):
            remote(rr.at[odd, me_r], rr.at[odd, me_r], k_rr, row_peer(d)[1]).start()

        @pl.when(is_owner)
        def _():
            rc[me_c] = pb_send[me_o]
            wait_all(rc, 3, some_col)
            total = rc[0]
            for q in range(1, npc):
                total = total + rc[q]
            gb[me_o] = total
            for d in range(1, npc):
                remote(gb.at[me_o], gb.at[me_o], 2, col_peer(d)[1]).start()

        wait_all(rr.at[odd], k_rr, some_row)
        for g in range(nx):
            parts = [rr[odd, c * nwin + 2 * g + k, rank : rank + 8] for c in range(ncol) for k in range(2)]
            zs[odd, row, g * 8 : (g + 1) * 8] = functools.reduce(jnp.add, parts)
        for d in range(1, nrow):
            remote(zs.at[odd, row], zs.at[odd, row], k_zs, z_peer(d)[1]).start()

        sum_c = jnp.sum(c_now[...], axis=0, keepdims=True)
        sum_b = zs[odd, row, local_wins : local_wins + 1]
        rows = jnp.where(row_at == 0, 0.5 / (sum_b * sum_c), 0.0)
        norm_a = jnp.broadcast_to(jnp.transpose(rows)[:rank, 0:1], (rank, items))
        total = rr[odd, 0, 0:rank]
        for q in range(1, npr):
            total = total + rr[odd, q, 0:rank]
        a_now[...] = a * (0.5 + norm_a * total)

        wait_all(zs.at[odd], k_zs, some_z)
        stat = zs[odd, 0]
        for q in range(1, nrow):
            stat = stat + zs[odd, q]
        sum_b = stat[local_wins : local_wins + 1] * (1.0 / nrow)
        sum_a = stat[local_wins + 1 : local_wins + 2] * (1.0 / (2 * ncol))
        norm_c = 0.5 / (sum_a * sum_b)
        valid = lax.broadcasted_iota(jnp.int32, (local_wins, LANES), 1) < rank
        for g in range(nx):
            at = slice(g * local_wins, (g + 1) * local_wins)
            old = c_now[at, :]
            terms = old * stat[g * 8 : g * 8 + local_wins]
            c_now[at, :] = jnp.where(valid, old * (0.5 + norm_c * terms), 0.0)
        put_cols(0.5 / (sum_a * sum_c))
        norm_b = jnp.broadcast_to(cols_now[:, local_wins : local_wins + 1], (rank, items))
        tile[0:rank, :] = norm_b
        prepare()

        @pl.when(is_owner)
        def _():
            wait_all(gb, 2, some_col, npo - 1)

        @pl.when(not_owner)
        def _():
            wait_all(gb, 2, some_col, npo)

        for o in range(npo):
            g, top = o % groups, (o // groups) * rk_c
            at, over = slice(top, top + rk_c), slice(g * LANES, (g + 1) * LANES)
            b_now[at, over] = b_now[at, over] * (0.5 + tile[at, :] * gb[o])

        @pl.when(is_owner)
        def _():
            wait_sent(pb_send, 3, some_col, npo - 1)
            wait_sent(rc, 2, some_col)

        @pl.when(not_owner)
        def _():
            wait_sent(pb_send, 3, some_col, npo)

        wait_sent(rr.at[odd], k_rr, some_row)
        wait_sent(zs.at[odd], k_zs, some_z)
        return carry

    put_cols(jnp.zeros((1, LANES), F32))
    prepare()
    lax.fori_loop(0, STEPS, step, 0)

    shift = (LANES - me_r * row_width) % LANES
    rows = jnp.concatenate([pltpu.roll(a_now[...], shift, 1), pad], axis=0)
    row_out[...] = jnp.transpose(rows)[:row_width, :rank]
    block = b_now[:, 0:LANES]
    for g in range(1, groups):
        block = jnp.where(me_c // per == g, b_now[:, g * LANES : (g + 1) * LANES], block)
    shift = (LANES - (me_c % per) * col_width) % LANES
    col_out[...] = pltpu.roll(block, shift, 1)[:, :col_width]
    win_out[...] = c_now[pl.ds(win * own_wins, own_wins), :][:, :rank]


def local(sizes, counts, rows, cols, wins):
    nrow, ncol, nwin = sizes
    rank, row_width = rows.shape
    own_wins, items, columns = counts.shape
    half = columns // 2
    nx = nwin // 2
    npr, npc = ncol * nwin, nrow * nx
    npo = (nrow // 2) * nx
    rk_c = rank * (half // LANES) // npo
    vmem = lambda *shape, dtype=F32: pltpu.VMEM(shape, dtype)
    spec = pl.BlockSpec(memory_space=pltpu.VMEM)
    args = (counts, rows.T, cols, wins.T)
    out = pl.pallas_call(
        functools.partial(kernel, sizes),
        out_shape=[jax.ShapeDtypeStruct(v.shape, F32) for v in args[1:]],
        in_specs=[pl.BlockSpec(memory_space=pl.ANY)] + [spec] * 3,
        out_specs=[spec] * 3,
        scratch_shapes=[
            vmem(*counts.shape, dtype=jnp.int32),
            vmem(2 * own_wins * items, half),
            vmem(own_wins * items, half),
            vmem(rank, items),
            vmem(rank, half),
            vmem(nwin * own_wins, LANES),
            vmem(rank, LANES),
            vmem(2 * own_wins * items, 4 * rank, dtype=BF16),
            vmem(rank, 2 * own_wins * items, dtype=BF16),
            vmem(rank, 2 * own_wins * items, dtype=BF16),
            vmem(LANES, LANES),
            vmem(npr, rank, LANES),
            vmem(npc, rank, LANES),
            vmem(2, npr, rank + 8, LANES),
            vmem(npo, rk_c, LANES),
            vmem(npc, rk_c, LANES),
            vmem(npo, rk_c, LANES),
            vmem(2, nrow, 8 * nx, LANES),
            pltpu.SemaphoreType.DMA((2, 9)),
            pltpu.SemaphoreType.DMA,
        ],
        compiler_params=pltpu.CompilerParams(
            collective_id=0, has_side_effects=True, vmem_limit_bytes=60 * 1024 * 1024
        ),
    )(*args)
    return out[0].T, out[1], out[2].T


def solution(mesh):
    in_specs = (
        P("win", "row", "col"),
        P(None, ("row", "col", "win")),
        P(None, ("col", "row", "win")),
        P(None, "win"),
    )
    out_specs = (P(None, ("row", "col", "win")), P(None, ("col", "row", "win")), P(None, "win"))
    sizes = (mesh.shape["row"], mesh.shape["col"], mesh.shape["win"])
    return jax.shard_map(
        functools.partial(local, sizes), mesh=mesh, in_specs=in_specs, out_specs=out_specs, check_vma=False
    )
```

time: 55 us -> 52.5 us (0.955)
  local copies, waits for them, and re-layouts: 4.01 us -> 2.5 us
  Pallas kernels: 50.1 us -> 49 us
    pallas_call x2 -> x0, local copies, waits for them, and re-layouts: 1.3 us -> none  [local(): pl.pallas_call(functools.partial(kernel, sizes), out_shape=[jax.ShapeDtyp...]
    pallas_call x1, Pallas kernels: 50.1 us -> 49 us  [local(): pl.pallas_call(functools.partial(kernel, sizes), out_shape=[jax.ShapeDtyp...]
    unnamed x9 -> x7, local copies, waits for them, and re-layouts: 2.71 us -> 2.5 us
where the time goes in v2:
time: 52.5 us; the launch traced here: 52.2 us
  Pallas kernels  49 us (93%)
  local copies, waits for them, and re-layouts  2.5 us (5%)
  between operations  0.65 us (1%)
    pallas_call x1, Pallas kernels, local(): pl.pallas_call(functools.partial(kernel, sizes), out_shape=[jax.ShapeDtyp...  49 us
    unnamed x7, local copies, waits for them, and re-layouts  2.5 us

profile of v2, /device:TPU:0, one launch (start us, length us, event | category | flops | bytes accessed | tf_op | source)
XLA Modules:
  0.0 52.2 jit_solution(10534269323316399028)
XLA Ops:
  0.6 49.0 %shard_map.67 = (f32[16,32]{1,0:T(8,128)}, f32[32,64]{1,0:T(8,128)}, f32[2,32]{1,0:T(2,128)}) custom-call(s32[2,128,1024]{2,1,0:T(8,128)} %counts_ref.1, f32[16,32]{1,0:T(8,128)} %bitcast.4, f32[32,64]{1,0:T(8,128)} %col_ref.1, f32[2,32]{1,0:T(2,128)} %bitcast.6), custom_call_target="tpu_custom_call" | custom-call | tf_op jit(solution)/shard_map/pallas_call | solution.py:316
  49.7 0.0 copy-start
  49.7 1.3 %copy.10 = f32[32,16]{0,1:T(8,128)} copy(f32[32,16]{0,1:T(8,128)} %bitcast.5) | data formatting | bytes 4096
  51.0 0.0 copy-done
  51.0 0.0 copy-start.1
  51.0 0.6 %copy.11 = f32[32,64]{1,0:T(8,128)} copy(f32[32,64]{1,0:T(8,128)S(1)} %copy-done) | data formatting | bytes 16384
  51.6 0.0 copy-done.1
  51.6 0.6 %copy.12 = f32[32,2]{0,1:T(2,128)} copy(f32[32,2]{0,1:T(2,128)S(1)} %bitcast.7) | data formatting | bytes 512
Async XLA Ops:
  49.7 1.3 %copy-start = (f32[32,64]{1,0:T(8,128)S(1)}, f32[32,64]{1,0:T(8,128)}, u32[]{:S(2)}) copy-start(f32[32,64]{1,0:T(8,128)} %get-tuple-element.13) | copy-start | bytes 24580
  51.0 0.6 %copy-start.1 = (f32[2,32]{1,0:T(2,128)S(1)}, f32[2,32]{1,0:T(2,128)}, u32[]{:S(2)}) copy-start(f32[2,32]{1,0:T(2,128)} %get-tuple-element.8) | copy-start | bytes 772

commit v3 on v2

--- a/solution.py
+++ b/solution.py
@@ -29,7 +29,7 @@
     counts_ref, row_ref, col_ref, win_ref,
     row_out, col_out, win_out,
     counts_here, cnt, cnt_send, a_now, b_now, c_now, cols_now, left_now, high_now, low_now, tile,
-    ia, ib, rr, pb_send, rc, gb, zs,
+    ia, ib, rr, sr, pb_send, rc, gb, zs,
     sems, load_sem,
 ):
     nrow, ncol, nwin = sizes
@@ -96,13 +96,6 @@
     ia[me_r] = jnp.transpose(tile[...])[:rank]
     ib[me_c] = jnp.zeros((rank, LANES), F32)
     ib[me_c, :, 0:col_width] = col_ref[...]
-
-    pl.semaphore_wait(barrier, npr - 1 + npc - 1)
-
-    for d in range(1, npc):
-        remote(ib.at[me_c], ib.at[me_c], 0, col_peer(d)[1]).start()
-    for d in range(1, npr):
-        remote(ia.at[me_r], ia.at[me_r], 1, row_peer(d)[1]).start()
 
     span = 2 * LANES
     src_at = lax.broadcasted_iota(jnp.int32, (span, span), 0)
@@ -121,6 +114,13 @@
             at = pl.ds(pl.multiple_of(base + w * items, items), items)
             cnt[at, g * LANES : (g + 1) * LANES] = moved[:, :LANES]
             cnt_send[w * items : (w + 1) * items, g * LANES : (g + 1) * LANES] = moved[:, LANES:]
+    pl.semaphore_wait(barrier, npr - 1 + npc - 1)
+
+    for d in range(1, npc):
+        remote(ib.at[me_c], ib.at[me_c], 0, col_peer(d)[1]).start()
+    for d in range(1, npr):
+        remote(ia.at[me_r], ia.at[me_r], 1, row_peer(d)[1]).start()
+
     mine = cnt.at[pl.ds(pl.multiple_of(base, items), own_wins * items)]
     swap = remote(cnt_send, mine, 8, partner)
     swap.start()
@@ -177,7 +177,7 @@
 
     def step(index, carry):
         odd = index % 2
-        k_rr, k_zs = 4 + odd, 6 + odd
+        k_rr, k_zs, k_sr = 4 + odd, 6 + odd, 9 + odd
         b = b_now[...]
         b_high, b_low = split(b)
         right = jnp.concatenate([b_high, b_low, b_high, b_low], axis=0)
@@ -210,8 +210,10 @@
             stats = jnp.where(lane_at == w, jnp.sum(part * a, axis=1, keepdims=True), stats)
         stats = jnp.where(lane_at == local_wins, jnp.sum(b, axis=1, keepdims=True), stats)
         stats = jnp.where(lane_at == local_wins + 1, jnp.sum(a, axis=1, keepdims=True), stats)
-        rr[odd, me_r, 0:rank] = pa
-        rr[odd, me_r, rank : rank + 8] = jnp.transpose(jnp.concatenate([stats, pad], axis=0))[:8]
+        sr[odd, me_r] = jnp.transpose(jnp.concatenate([stats, pad], axis=0))[:8]
+        for d in range(1, npr):
+            remote(sr.at[odd, me_r], sr.at[odd, me_r], k_sr, row_peer(d)[1]).start()
+        rr[odd, me_r] = pa
         for d in range(1, npr):
             remote(rr.at[odd, me_r], rr.at[odd, me_r], k_rr, row_peer(d)[1]).start()
 
@@ -226,9 +228,9 @@
             for d in range(1, npc):
                 remote(gb.at[me_o], gb.at[me_o], 2, col_peer(d)[1]).start()
 
-        wait_all(rr.at[odd], k_rr, some_row)
+        wait_all(sr.at[odd], k_sr, some_row)
         for g in range(nx):
-            parts = [rr[odd, c * nwin + 2 * g + k, rank : rank + 8] for c in range(ncol) for k in range(2)]
+            parts = [sr[odd, c * nwin + 2 * g + k] for c in range(ncol) for k in range(2)]
             zs[odd, row, g * 8 : (g + 1) * 8] = functools.reduce(jnp.add, parts)
         for d in range(1, nrow):
             remote(zs.at[odd, row], zs.at[odd, row], k_zs, z_peer(d)[1]).start()
@@ -237,9 +239,10 @@
         sum_b = zs[odd, row, local_wins : local_wins + 1]
         rows = jnp.where(row_at == 0, 0.5 / (sum_b * sum_c), 0.0)
         norm_a = jnp.broadcast_to(jnp.transpose(rows)[:rank, 0:1], (rank, items))
-        total = rr[odd, 0, 0:rank]
+        wait_all(rr.at[odd], k_rr, some_row)
+        total = rr[odd, 0]
         for q in range(1, npr):
-            total = total + rr[odd, q, 0:rank]
+            total = total + rr[odd, q]
         a_now[...] = a * (0.5 + norm_a * total)
 
         wait_all(zs.at[odd], k_zs, some_z)
@@ -283,6 +286,7 @@
             wait_sent(pb_send, 3, some_col, npo)
 
         wait_sent(rr.at[odd], k_rr, some_row)
+        wait_sent(sr.at[odd], k_sr, some_row)
         wait_sent(zs.at[odd], k_zs, some_z)
         return carry
 
@@ -299,6 +303,11 @@
     shift = (LANES - (me_c % per) * col_width) % LANES
     col_out[...] = pltpu.roll(block, shift, 1)[:, :col_width]
     win_out[...] = c_now[pl.ds(win * own_wins, own_wins), :][:, :rank]
+
+
+def hand_on(*refs):
+    for source, target in zip(refs[:3], refs[3:]):
+        target[...] = source[...]
 
 
 def local(sizes, counts, rows, cols, wins):
@@ -332,18 +341,25 @@
             vmem(LANES, LANES),
             vmem(npr, rank, LANES),
             vmem(npc, rank, LANES),
-            vmem(2, npr, rank + 8, LANES),
+            vmem(2, npr, rank, LANES),
+            vmem(2, npr, 8, LANES),
             vmem(npo, rk_c, LANES),
             vmem(npc, rk_c, LANES),
             vmem(npo, rk_c, LANES),
             vmem(2, nrow, 8 * nx, LANES),
-            pltpu.SemaphoreType.DMA((2, 9)),
+            pltpu.SemaphoreType.DMA((2, 11)),
             pltpu.SemaphoreType.DMA,
         ],
         compiler_params=pltpu.CompilerParams(
             collective_id=0, has_side_effects=True, vmem_limit_bytes=60 * 1024 * 1024
         ),
     )(*args)
+    out = pl.pallas_call(
+        hand_on,
+        out_shape=[jax.ShapeDtypeStruct(v.shape, F32) for v in args[1:]],
+        in_specs=[spec] * 3,
+        out_specs=[spec] * 3,
+    )(*out)
     return out[0].T, out[1], out[2].T
 
 

time: 52.5 us -> 51.1 us (0.973)
  local copies, waits for them, and re-layouts: 2.5 us -> 0 us
  Pallas kernels: 49 us -> 50.1 us
    unnamed x7 -> x0, local copies, waits for them, and re-layouts: 2.5 us -> none
    pallas_call x0 -> x1, Pallas kernels: none -> 1.33 us  [local(): pl.pallas_call(hand_on, out_shape=[jax.ShapeDtypeStruct(v.shape, F32) for...]
where the time goes in v3:
time: 51.1 us; the launch traced here: 50.7 us
  Pallas kernels  50.1 us (98%)
  between operations  0.64 us (1%)
    pallas_call x1, Pallas kernels, local(): pl.pallas_call(functools.partial(kernel, sizes), out_shape=[jax.ShapeDtyp...  48.8 us
    pallas_call x1, Pallas kernels, local(): pl.pallas_call(hand_on, out_shape=[jax.ShapeDtypeStruct(v.shape, F32) for...  1.33 us

profile of v3, /device:TPU:0, one launch (start us, length us, event | category | flops | bytes accessed | tf_op | source)
XLA Modules:
  0.0 50.7 jit_solution(1429972100273237651)
XLA Ops:
  0.6 48.8 %shard_map.67 = (f32[16,32]{1,0:T(8,128)}, f32[32,64]{1,0:T(8,128)}, f32[2,32]{1,0:T(2,128)}) custom-call(s32[2,128,1024]{2,1,0:T(8,128)} %counts_ref.1, f32[16,32]{1,0:T(8,128)} %bitcast.4, f32[32,64]{1,0:T(8,128)} %col_ref.1, f32[2,32]{1,0:T(2,128)} %bitcast.5), custom_call_target="tpu_custom_call" | custom-call | tf_op jit(solution)/shard_map/pallas_call | solution.py:325
  49.4 1.3 %shard_map.68 = (f32[16,32]{1,0:T(8,128)}, f32[32,64]{1,0:T(8,128)}, f32[2,32]{1,0:T(2,128)}) custom-call(f32[16,32]{1,0:T(8,128)} %get-tuple-element.9.refs_0_, f32[32,64]{1,0:T(8,128)} %get-tuple-element.10.refs_1_, f32[2,32]{1,0:T(2,128)} %get-tuple-element.11.refs_2_), custom_call_target="tpu_custom_call" | custom-call | tf_op jit(solution)/shard_map/pallas_call | solution.py:357
